TPU v7x, 32 devices: a whole 2x2x4 slice. The times are simulated.
32 devices in a mesh: row: 8 (over y, x, core), col: 4 (over z).
Axes of the slice: x: 2, y: 2, z: 4, core: 2. Of those that a mesh axis runs over, the one named last changes fastest.
Arguments:
- tile_values: bfloat16 [3072, 256, 256], P(('row', 'col')), may hold values from -0.375 to 0.375
- tile_coords: int32 [3072, 2], P(('row', 'col')), may hold values from 0 to 15, as said below
- live_counts: int32 [32], P(('row', 'col')), may hold values from 24 to 96, as said below
Outputs:
- range_basis: float32 [32768, 192], P(('row', 'col'))
- projected: float32 [4, 4096, 192], P('col', 'row')
Inputs may be any that keep to these rules, and one draw needn't show every extreme that they name: `tile_coords`: for each device, column 0 is below 16, column 1 is below 16, and the 96 positions of its slots are distinct. `live_counts`: some device has all 96 slots live.
All inputs are finite; a program needn't handle non-finite values.
Results may differ from a plain program's by a relative error of at most 0.0003.
Values sent between devices are 32-bit elements; how exact they have to be, the bound alone decides.
A program may use at most 128 MiB of HBM per device.

v0:
```python
import math

import jax
import jax.numpy as jnp
from jax import lax
from jax.sharding import PartitionSpec as P

TB = 256
K = 192
RT = 16
CT = 16


def sketch_signs(column_ids, rank_cols):
    rank_index = jnp.arange(rank_cols, dtype=jnp.int32)
    hashed = column_ids[..., None] * rank_cols + rank_index
    hashed = hashed * 747796405 + 1442695040
    hashed = hashed ^ hashed >> 15
    hashed = hashed * 1103515245 + 12345
    hashed = hashed ^ hashed >> 13
    return (1 - 2 * (hashed >> 9 & 1)).astype(jnp.float32)


def basis_from(sketch_rows, gram_matrix, basis_scale):
    factor = jnp.linalg.cholesky(gram_matrix)
    solved = jax.scipy.linalg.solve_triangular(factor, sketch_rows.T, lower=True)
    return basis_scale * solved.T


def per_device(tile_values, tile_coords, live_counts):
    slot_count = tile_values.shape[0]
    col_index = lax.axis_index("col")
    tile_row = tile_coords[:, 0]
    tile_col = tile_coords[:, 1]
    live_mask = (jnp.arange(slot_count, dtype=jnp.int32) < live_counts[0]).astype(jnp.float32)[
        :, None, None
    ]
    column_ids = (
        col_index * (CT * TB) + tile_col[:, None] * TB + jnp.arange(TB, dtype=jnp.int32)[None, :]
    )
    test_signs = sketch_signs(column_ids, K).astype(jnp.bfloat16)
    sketch_terms = (
        jnp.einsum("tij,tjk->tik", tile_values, test_signs, preferred_element_type=jnp.float32)
        * live_mask
    )
    sketch_part = jax.ops.segment_sum(sketch_terms, tile_row, num_segments=RT).reshape(RT * TB, K)
    basis_scale = math.sqrt(RT * TB * lax.axis_size("row"))
    sketch_full = lax.psum(sketch_part, "col")
    gram_local = jnp.dot(
        sketch_full.T,
        sketch_full,
        precision=lax.Precision.HIGHEST,
        preferred_element_type=jnp.float32,
    )
    gram_matrix = lax.psum(gram_local, "row")
    basis_full = basis_from(sketch_full, gram_matrix, basis_scale)
    share_rows = RT * TB // lax.axis_size("col")
    range_basis = lax.dynamic_slice_in_dim(basis_full, col_index * share_rows, share_rows, 0)
    picked = basis_full.reshape(RT, TB, K)[tile_row]
    adjoint_terms = (
        jnp.einsum(
            "tij,tik->tjk",
            tile_values,
            picked,
            precision=lax.Precision.HIGHEST,
            preferred_element_type=jnp.float32,
        )
        * live_mask
    )
    adjoint_part = jax.ops.segment_sum(adjoint_terms, tile_col, num_segments=CT).reshape(CT * TB, K)
    projected = lax.psum_scatter(adjoint_part, "row", scatter_dimension=0, tiled=True)
    return (range_basis, projected[None])


def solution(mesh):
    in_specs = (P(("row", "col"), None, None), P(("row", "col"), None), P(("row", "col")))
    out_specs = (P(("row", "col"), None), P("col", "row", None))
    return jax.shard_map(
        per_device, mesh=mesh, in_specs=in_specs, out_specs=out_specs, check_vma=False
    )
```

profile of v0, /device:TPU:0, one launch (start us, length us, event | category | flops | bytes accessed | tf_op | source)
XLA Modules:
  0.0 415.5 jit_solution(4421411043517369769)
XLA Ops:
  7.2 0.0 all-reduce.6.cloned.1.call-start
  7.2 0.8 fusion.31
  8.0 0.1 add_multiply_fusion
  8.7 16.9 %multiply_bitcast_fusion.1 = f32[96,256,192]{1,2,0:T(8,128)} fusion(f32[96]{0:T(128)S(1)} %compare_convert_fusion, bf16[96,256,256]{2,1,0:T(8,128)(2,1)} %param.3, s32[96,256]{1,0:T(8,128)S(1)} %add_multiply_fusion), kind=kOutput, calls=%fused_computation.14 | convolution fusion | flops 2491416576 | bytes 31555968 | tf_op jit(solution)/shard_map/tij,tjk->tik/dot_general | solution.py:43
  25.6 0.3 broadcast.151.clone
  25.9 29.1 %scatter_fusion = f32[16,256,192]{1,2,0:T(8,128)S(1)} fusion(f32[16,256,192]{1,2,0:T(8,128)S(1)} %broadcast.151.clone, s32[96]{0:T(128)S(1)} %get-tuple-element.29, f32[96,256,192]{1,2,0:T(8,128)} %multiply_bitcast_fusion.1), kind=kCustom, calls=%fused_computation.1 | custom fusion | flops 4718592 | bytes 56623488 | tf_op jit(solution)/shard_map/scatter-add | solution.py:46
  55.0 2.1 copy.14
  57.1 0.0 all-reduce.6.cloned.1.call-update
  57.1 0.0 all-reduce.8.cloned.1.call-start
  57.2 123.9 %all-reduce.6.cloned.1.call-done = f32[4096,192]{0,1:T(8,128)} async-done(((f32[4096,192]{0,1:T(8,128)}), f32[4096,192]{0,1:T(8,128)}) %all-reduce.6.cloned.1.call-update) | async-done | bytes 3145744 | tf_op jit(solution)/shard_map/psum | solution.py:48
  181.1 6.2 %fusion.41 = f32[192,192]{0,1:T(8,128)} fusion(f32[4096,192]{0,1:T(8,128)} %all-reduce.6.cloned.1.call-done), kind=kOutput, calls=%fused_computation.78 | convolution fusion | flops 1811939328 | bytes 3293184 | tf_op jit(solution)/shard_map/dot_general | solution.py:49
  187.3 0.0 all-reduce.8.cloned.1.call-update
  187.3 0.2 reduce-scatter.2.cloned.1.call-start
  187.5 52.3 %all-reduce.8.cloned.1.call-done = f32[192,192]{0,1:T(8,128)} async-done(((f32[192,192]{0,1:T(8,128)}), f32[192,192]{0,1:T(8,128)}) %all-reduce.8.cloned.1.call-update) | async-done | bytes 147472 | tf_op jit(solution)/shard_map/psum | solution.py:55
  239.8 1.0 copy.9
  240.9 1.0 fusion.24
  241.8 11.7 %cholesky.51 = f32[128,128]{1,0:T(8,128)S(1)} custom-call(f32[128,128]{1,0:T(8,128)S(1)} %cholesky.124), custom_call_target="Cholesky" | custom-call | tf_op jit(solution)/shard_map/jit(cholesky)/cholesky | solution.py:25
  253.6 9.8 %custom-call.15 = f32[1,128,128]{1,2,0:T(8,128)S(1)} custom-call(f32[1,128,128]{2,1,0:T(8,128)S(1)} %get-tuple-element.23), custom_call_target="InvertDiagBlocksLowerTriangular" | custom-call | tf_op jit(solution)/shard_map/jit(cholesky)/cholesky | solution.py:25
  263.4 0.2 constant_dynamic-update-slice_fusion.1
  263.6 0.2 convolution_subtract_fusion.1
  263.8 5.8 %cholesky.110 = f32[64,64]{1,0:T(8,128)S(1)} custom-call(f32[64,64]{1,0:T(8,128)S(1)} %convolution_subtract_fusion.1), custom_call_target="Cholesky" | custom-call | tf_op jit(solution)/shard_map/jit(cholesky)/cholesky | solution.py:25
  269.7 0.6 compare_reduce_fusion
  270.3 0.6 compare_reduce_fusion.1
  272.3 0.1 fusion.25
  272.4 19.9 %custom-call.16 = f32[2,128,128]{1,2,0:T(8,128)S(1)} custom-call(f32[2,128,128]{2,1,0:T(8,128)S(1)} %pad_maximum_fusion), custom_call_target="InvertDiagBlocksLowerTriangular" | custom-call | tf_op jit(solution)/shard_map/jit(_solve_triangular)/triangular_solve | solution.py:26
  292.3 3.5 fusion.22
  295.8 2.4 convolution_subtract_fusion
  298.3 1.0 fusion.29
  299.3 0.4 maximum_multiply_fusion
  299.7 0.0 copy-start
  299.7 1.6 copy-done
  301.3 0.3 copy.17
  301.7 8.2 %gather_fusion = f32[96,256,192]{1,2,0:T(8,128)} fusion(f32[16,256,192]{1,2,0:T(8,128)S(1)} %bitcast.57, s32[1024]{0:T(1024)S(1)} %pad_clamp_fusion), kind=kCustom, calls=%fused_computation | custom fusion | bytes 37749120 | tf_op jit(solution)/shard_map/gather | solution.py:59
  309.9 21.8 %multiply_bitcast_fusion = f32[96,256,192]{1,2,0:T(8,128)} fusion(f32[96]{0:T(128)S(1)} %compare_convert_fusion, f32[96,256,192]{1,2,0:T(8,128)} %gather_fusion, bf16[96,256,256]{2,1,0:T(8,128)(2,1)} %param.3), kind=kOutput, calls=%fused_computation.13 | convolution fusion | flops 14500233216 | bytes 50332032 | tf_op jit(solution)/shard_map/tij,tik->tjk/dot_general | solution.py:61
  331.7 0.3 broadcast.151
  332.0 29.1 %scatter_fusion.1 = f32[16,256,192]{1,2,0:T(8,128)S(1)} fusion(f32[16,256,192]{1,2,0:T(8,128)S(1)} %broadcast.151, s32[96]{0:T(128)S(1)} %get-tuple-element.27, f32[96,256,192]{1,2,0:T(8,128)} %multiply_bitcast_fusion), kind=kCustom, calls=%fused_computation.2 | custom fusion | flops 4718592 | bytes 56623488 | tf_op jit(solution)/shard_map/scatter-add | solution.py:70
  361.1 2.1 copy.15
  363.2 0.0 reduce-scatter.2.cloned.1.call-update
  363.2 2.1 dynamic-slice_bitcast_fusion
  365.3 43.7 %reduce-scatter.2.cloned.1.call-done = f32[512,192]{0,1:T(8,128)} async-done(((f32[4096,192]{0,1:T(8,128)}), f32[512,192]{0,1:T(8,128)}) %reduce-scatter.2.cloned.1.call-update) | async-done | bytes 393232 | tf_op jit(solution)/shard_map/reduce_scatter | solution.py:71
  (11 shorter events, 0.2 us)
Async XLA Ops:
  7.2 173.9 %all-reduce.6.cloned.1.call-start = ((), (), s32[]{:S(2)}) async-start(), calls=%async_computation.1 | async-start | bytes 6291456 | tf_op jit(solution)/shard_map/psum | solution.py:48
  57.1 182.7 %all-reduce.8.cloned.1.call-start = ((), (), s32[]{:S(2)}) async-start(), calls=%async_computation.2 | async-start | bytes 393216 | tf_op jit(solution)/shard_map/psum | solution.py:55
  187.3 221.7 %reduce-scatter.2.cloned.1.call-start = ((), (), s32[]{:S(2)}) async-start(), calls=%async_computation.3 | async-start | bytes 3538944 | tf_op jit(solution)/shard_map/reduce_scatter | solution.py:71
  299.7 1.6 copy-start
Sparse Core Ops, SparseCore 0:
  57.2 123.7 all-reduce.5
  187.4 52.3 all-reduce.7
  363.3 45.6 reduce-scatter.1
where the time goes:
time: 416 us; the launch traced here: 415 us
  waiting for transfers between devices  220 us (53%)
  other arithmetic  109 us (26%)
  matrix products  52.2 us (13%)
  local copies, waits for them, and re-layouts  18.1 us (4%)
  between operations  15.9 us (4%)
    psum x1, waiting for transfers between devices, per_device(): sketch_full = lax.psum(sketch_part, 'col')  124 us
    psum x1, waiting for transfers between devices, per_device(): gram_matrix = lax.psum(gram_local, 'row')  52.3 us
    reduce_scatter x1, waiting for transfers between devices, per_device(): lax.psum_scatter(adjoint_part, 'row', scatter_dimension=0, tiled=True)  43.7 us
    scatter-add x1, other arithmetic, per_device(): jax.ops.segment_sum(adjoint_terms, tile_col, num_segments=CT)  29.1 us
    scatter-add x1, other arithmetic, per_device(): jax.ops.segment_sum(sketch_terms, tile_row, num_segments=RT)  29.1 us
    another operation x7, other arithmetic, basis_from(): factor = jnp.linalg.cholesky(gram_matrix)  28.7 us
    dot_general x1, matrix products, per_device(): jnp.einsum('tij,tik->tjk', tile_values, picked, precision=lax.Precision.H...  21.8 us
    another operation x6, other arithmetic, basis_from(): jax.scipy.linalg.solve_triangular(factor, sketch_rows.T, lower=True)  20 us
  transfers between devices with their start and end apart: 3, of which 3 were waited for; matrix products, arithmetic and copies ran while one was open for 1% of the time, Pallas kernels for 0%

commit v1 on v0

v1 whole, which is shorter than its diff:
```python
import functools
import math

import jax
import jax.numpy as jnp
from jax import lax
from jax.experimental import pallas as pl
from jax.experimental.pallas import tpu as pltpu
from jax.sharding import PartitionSpec as P

K = 192
RT = 16
CT = 16
CHUNKS = 12
HIGHEST = lax.Precision.HIGHEST


def load_tiles(tiles_hbm, tiles, sems):
    per = tiles.shape[0] // CHUNKS
    return [
        pltpu.make_async_copy(
            tiles_hbm.at[pl.ds(c * per, per)], tiles.at[pl.ds(c * per, per)], sems.at[c]
        )
        for c in range(CHUNKS)
    ]


def sketch_kernel(coords, live, base, tiles_hbm, out, tiles, signs, sems):
    tb = tiles.shape[1]
    copies = load_tiles(tiles_hbm, tiles, sems)
    for copy in copies:
        copy.start()
    out[...] = jnp.zeros_like(out)

    def make_signs(j, carry):
        column = lax.broadcasted_iota(jnp.int32, (K, tb), 1) + (base[0] + j * tb)
        h = column * K + lax.broadcasted_iota(jnp.int32, (K, tb), 0)
        h = h * 747796405 + 1442695040
        h = h ^ (h >> 15)
        h = h * 1103515245 + 12345
        h = h ^ (h >> 13)
        signs[j] = (1 - 2 * ((h >> 9) & 1)).astype(jnp.float32).astype(jnp.bfloat16)
        return carry

    lax.fori_loop(0, CT, make_signs, 0)
    per = tiles.shape[0] // CHUNKS
    for c, copy in enumerate(copies):
        copy.wait()

        def step(s, carry):
            i = coords[s, 0]
            j = coords[s, 1]
            out[i] += lax.dot_general(
                signs[j], tiles[s], (((1,), (1,)), ((), ())), preferred_element_type=jnp.float32
            )
            return carry

        lax.fori_loop(c * per, jnp.minimum((c + 1) * per, live[0]), step, 0)


def adjoint_kernel(coords, live, tiles_hbm, sketch_hbm, out, tiles, sketch, parts, sems, sketch_sem):
    half = out.shape[2]
    sketch_copy = pltpu.make_async_copy(sketch_hbm, sketch, sketch_sem)
    sketch_copy.start()
    copies = load_tiles(tiles_hbm, tiles, sems)
    for copy in copies:
        copy.start()
    out[...] = jnp.zeros_like(out)
    sketch_copy.wait()

    def split(i, carry):
        x = sketch[i]
        for p in range(3):
            y = x.astype(jnp.bfloat16)
            parts[i, p * K : (p + 1) * K, :] = y
            x = x - y.astype(jnp.float32)
        return carry

    lax.fori_loop(0, RT, split, 0)
    per = tiles.shape[0] // CHUNKS
    for c, copy in enumerate(copies):
        copy.wait()

        def step(s, carry):
            i = coords[s, 0]
            j = coords[s, 1]
            t = jnp.dot(parts[i], tiles[s], preferred_element_type=jnp.float32)
            t = t[:K] + t[K : 2 * K] + t[2 * K :]
            out[2 * j] += t[:, :half]
            out[2 * j + 1] += t[:, half:]
            return carry

        lax.fori_loop(c * per, jnp.minimum((c + 1) * per, live[0]), step, 0)


SMEM = pl.BlockSpec(memory_space=pltpu.SMEM)
VMEM = pl.BlockSpec(memory_space=pltpu.VMEM)
ANY = pl.BlockSpec(memory_space=pl.ANY)


def sketch_call(tile_coords, live_counts, base, tile_values):
    slots, tb, _ = tile_values.shape
    return pl.pallas_call(
        sketch_kernel,
        out_shape=jax.ShapeDtypeStruct((RT, K, tb), jnp.float32),
        in_specs=[SMEM, SMEM, SMEM, ANY],
        out_specs=VMEM,
        scratch_shapes=[
            pltpu.VMEM((slots, tb, tb), jnp.bfloat16),
            pltpu.VMEM((CT, K, tb), jnp.bfloat16),
            pltpu.SemaphoreType.DMA((CHUNKS,)),
        ],
        compiler_params=pltpu.CompilerParams(vmem_limit_bytes=40 << 20),
        cost_estimate=pl.CostEstimate(
            flops=2 * slots * tb * tb * K, bytes_accessed=slots * tb * tb * 2, transcendentals=0
        ),
    )(tile_coords, live_counts, base, tile_values)


def adjoint_call(tile_coords, live_counts, tile_values, sketch_t):
    slots, tb, _ = tile_values.shape
    return pl.pallas_call(
        adjoint_kernel,
        out_shape=jax.ShapeDtypeStruct((2 * CT, K, tb // 2), jnp.float32),
        in_specs=[SMEM, SMEM, ANY, ANY],
        out_specs=VMEM,
        scratch_shapes=[
            pltpu.VMEM((slots, tb, tb), jnp.bfloat16),
            pltpu.VMEM((RT, K, tb), jnp.float32),
            pltpu.VMEM((RT, 3 * K, tb), jnp.bfloat16),
            pltpu.SemaphoreType.DMA((CHUNKS,)),
            pltpu.SemaphoreType.DMA,
        ],
        compiler_params=pltpu.CompilerParams(vmem_limit_bytes=48 << 20),
        cost_estimate=pl.CostEstimate(
            flops=6 * slots * tb * tb * K, bytes_accessed=slots * tb * tb * 2, transcendentals=0
        ),
    )(tile_coords, live_counts, tile_values, sketch_t)


def per_device(tile_values, tile_coords, live_counts):
    tb = tile_values.shape[1]
    base = (lax.axis_index("col") * (CT * tb)).reshape(1)
    scale = math.sqrt(RT * tb * lax.axis_size("row"))
    part = sketch_call(tile_coords, live_counts, base, tile_values)
    share = lax.psum_scatter(part, "col", scatter_dimension=0, tiled=True)
    full = lax.all_gather(share, "col", axis=0, tiled=True)
    gram = jnp.einsum(
        "bkn,bln->kl", share, share, precision=HIGHEST, preferred_element_type=jnp.float32
    )
    gram = lax.psum(gram, ("row", "col"))
    factor = jnp.linalg.cholesky(gram)
    inverse = scale * jax.scipy.linalg.solve_triangular(
        factor, jnp.eye(K, dtype=jnp.float32), lower=True
    )
    basis = jnp.einsum("bkn,lk->bnl", share, inverse, precision=HIGHEST).reshape(-1, K)
    adjoint = adjoint_call(tile_coords, live_counts, tile_values, full)
    mine = lax.psum_scatter(adjoint, "row", scatter_dimension=0, tiled=True)
    projected = jnp.einsum("bkn,lk->bnl", mine, inverse, precision=HIGHEST).reshape(1, -1, K)
    return basis, projected


def solution(mesh):
    in_specs = (P(("row", "col"), None, None), P(("row", "col"), None), P(("row", "col")))
    out_specs = (P(("row", "col"), None), P("col", "row", None))
    return jax.shard_map(
        per_device, mesh=mesh, in_specs=in_specs, out_specs=out_specs, check_vma=False
    )
```

time: 416 us -> 355 us (0.85)
  other arithmetic: 109 us -> 49.7 us
  matrix products: 52.2 us -> 6.67 us
  Pallas kernels: 0 us -> 38.3 us
  waiting for transfers between devices: 220 us -> 239 us
  local copies, waits for them, and re-layouts: 18.1 us -> 3.97 us
    psum x2 -> x1, waiting for transfers between devices: 176 us -> 106 us  [per_device(): gram = lax.psum(gram, ('row', 'col'))]
    all_gather x0 -> x1, waiting for transfers between devices: none -> 62.1 us  [per_device(): full = lax.all_gather(share, 'col', axis=0, tiled=True)]
    scatter-add x2 -> x0, other arithmetic: 58.2 us -> none  [the longest x1 29.1 us: per_device(): jax.ops.segment_sum(adjoint_terms, tile_col, num_segments=CT)]
    dot_general x3, matrix products: 44.8 us -> 5.36 us  [the longest x1 2.85 us: per_device(): jnp.einsum('bkn,bln->kl', share, share, precision=HIGHEST, preferred_elem...]
    pallas_call x0 -> x2, Pallas kernels: none -> 38.3 us  [the longest x1 22 us: adjoint_call(): pl.pallas_call(adjoint_kernel, out_shape=jax.ShapeDtypeStruct((2 * CT, K,...]
    reduce_scatter x1 -> x2, waiting for transfers between devices: 43.7 us -> 71.2 us  [the longest x1 71.2 us: per_device(): share = lax.psum_scatter(part, 'col', scatter_dimension=0, tiled=True)]
    gather x1 -> x0, local copies, waits for them, and re-layouts: 8.23 us -> none  [per_device(): picked = basis_full.reshape(RT, TB, K)[tile_row]]
    another operation x5, matrix products: 7.33 us -> 1.31 us  [the longest x3 0.94 us: per_device(): jax.scipy.linalg.solve_triangular(factor, jnp.eye(K, dtype=jnp.float32),...]
  transfers between devices with their start and end apart: 3 -> 4, of which waited for: 3 -> 3; matrix products, arithmetic and copies ran while one was open for 1% -> 16% of each run, Pallas kernels for 0% -> 6%
where the time goes in v1:
time: 355 us; the launch traced here: 354 us
  waiting for transfers between devices  239 us (67%)
  other arithmetic  49.7 us (14%)
  Pallas kernels  38.3 us (11%)
  between operations  15.9 us (4%)
  matrix products  6.67 us (2%)
  local copies, waits for them, and re-layouts  3.97 us (1%)
    psum x1, waiting for transfers between devices, per_device(): gram = lax.psum(gram, ('row', 'col'))  106 us
    reduce_scatter x1, waiting for transfers between devices, per_device(): share = lax.psum_scatter(part, 'col', scatter_dimension=0, tiled=True)  71.2 us
    all_gather x1, waiting for transfers between devices, per_device(): full = lax.all_gather(share, 'col', axis=0, tiled=True)  62.1 us
    another operation x7, other arithmetic, per_device(): factor = jnp.linalg.cholesky(gram)  28.7 us
    pallas_call x1, Pallas kernels, adjoint_call(): pl.pallas_call(adjoint_kernel, out_shape=jax.ShapeDtypeStruct((2 * CT, K,...  22 us
    another operation x6, other arithmetic, per_device(): jax.scipy.linalg.solve_triangular(factor, jnp.eye(K, dtype=jnp.float32),...  20 us
    pallas_call x1, Pallas kernels, sketch_call(): pl.pallas_call(sketch_kernel, out_shape=jax.ShapeDtypeStruct((RT, K, tb),...  16.4 us
  transfers between devices with their start and end apart: 4, of which 3 were waited for; matrix products, arithmetic and copies ran while one was open for 16% of the time, Pallas kernels for 6%

profile of v1, /device:TPU:0, one launch (start us, length us, event | category | flops | bytes accessed | tf_op | source)
XLA Modules:
  0.0 354.1 jit_solution(2472863032655599111)
XLA Ops:
  7.2 0.0 reduce-scatter.3.cloned.1.call-start
  7.9 0.8 copy.21.coords
  8.6 16.4 %shard_map.50 = f32[16,192,256]{2,1,0:T(8,128)} custom-call(s32[96,2]{1,0:T(8,128)S(1)} %copy.21.coords, s32[1]{0:T(128)S(6)} %copy.42.live, s32[1]{0:T(128)} %bitcast.base, bf16[96,256,256]{2,1,0:T(8,128)(2,1)} %tiles_hbm.3), custom_call_target="tpu_custom_call" | custom-call | flops 2415919104 | bytes 12582912 | tf_op jit(solution)/shard_map/pallas_call | solution.py:103
  25.0 0.0 reduce-scatter.3.cloned.1.call-update
  25.1 0.0 all-gather.2.cloned.1.call-start
  25.1 71.2 %reduce-scatter.3.cloned.1.call-done = f32[4,192,256]{2,1,0:T(8,128)} async-done(((f32[16,192,256]{2,1,0:T(8,128)}), f32[4,192,256]{2,1,0:T(8,128)}) %reduce-scatter.3.cloned.1.call-update) | async-done | bytes 786448 | tf_op jit(solution)/shard_map/reduce_scatter | solution.py:146
  96.3 0.0 all-gather.2.cloned.1.call-update
  96.3 0.0 all-reduce.5.cloned.1.call-start
  96.4 2.9 convolution_bitcast_fusion.1
  99.2 0.0 all-reduce.5.cloned.1.call-update
  99.3 0.0 reduce-scatter.5.cloned.1.call-start
  99.3 62.1 %all-gather.2.cloned.1.call-done.sketch_hbm = f32[16,192,256]{2,1,0:T(8,128)} async-done(((f32[4,192,256]{2,1,0:T(8,128)}), f32[16,192,256]{2,1,0:T(8,128)}) %all-gather.2.cloned.1.call-update) | async-done | bytes 3145744 | tf_op jit(solution)/shard_map/all_gather | solution.py:147
  161.4 22.0 %shard_map.51 = f32[32,192,128]{2,1,0:T(8,128)} custom-call(s32[96,2]{1,0:T(8,128)S(1)} %copy.21.coords, s32[1]{0:T(128)S(6)} %copy.42.live, bf16[96,256,256]{2,1,0:T(8,128)(2,1)} %tiles_hbm.3, f32[16,192,256]{2,1,0:T(8,128)} %all-gather.2.cloned.1.call-done.sketch_hbm), custom_call_target="tpu_custom_call" | custom-call | flops 7247757312 | bytes 12582912 | tf_op jit(solution)/shard_map/pallas_call | solution.py:122
  183.4 0.0 copy-start
  183.4 0.0 reduce-scatter.5.cloned.1.call-update
  183.5 106.0 %all-reduce.5.cloned.1.call-done = f32[192,192]{0,1:T(8,128)} async-done(((f32[192,192]{0,1:T(8,128)}), f32[192,192]{0,1:T(8,128)}) %all-reduce.5.cloned.1.call-update) | async-done | bytes 147472 | tf_op jit(solution)/shard_map/psum | solution.py:151
  289.4 1.0 copy.23
  290.5 1.0 fusion.1
  291.5 11.7 %cholesky.51 = f32[128,128]{1,0:T(8,128)S(1)} custom-call(f32[128,128]{1,0:T(8,128)S(1)} %cholesky.124), custom_call_target="Cholesky" | custom-call | tf_op jit(solution)/shard_map/jit(cholesky)/cholesky | solution.py:152
  303.2 9.8 %custom-call.15 = f32[1,128,128]{1,2,0:T(8,128)S(1)} custom-call(f32[1,128,128]{2,1,0:T(8,128)S(1)} %get-tuple-element.23), custom_call_target="InvertDiagBlocksLowerTriangular" | custom-call | tf_op jit(solution)/shard_map/jit(cholesky)/cholesky | solution.py:152
  313.0 0.2 constant_dynamic-update-slice_fusion.1
  313.2 0.2 convolution_subtract_fusion.1
  313.4 5.8 %cholesky.110 = f32[64,64]{1,0:T(8,128)S(1)} custom-call(f32[64,64]{1,0:T(8,128)S(1)} %convolution_subtract_fusion.1), custom_call_target="Cholesky" | custom-call | tf_op jit(solution)/shard_map/jit(cholesky)/cholesky | solution.py:152
  319.3 0.6 compare_reduce_fusion.1
  320.0 0.6 compare_reduce_fusion
  321.9 0.1 fusion.9
  322.0 19.9 %custom-call.16 = f32[2,128,128]{1,2,0:T(8,128)S(1)} custom-call(f32[2,128,128]{2,1,0:T(8,128)S(1)} %pad_maximum_fusion), custom_call_target="InvertDiagBlocksLowerTriangular" | custom-call | tf_op jit(solution)/shard_map/jit(_solve_triangular)/triangular_solve | solution.py:153
  341.9 0.3 fusion.5
  342.2 0.3 convolution_subtract_fusion
  342.5 0.3 fusion.13
  342.9 0.0 copy-done
  342.9 0.9 convolution_bitcast_fusion
  343.8 1.0 copy.37
  344.7 0.0 reduce-scatter.5.cloned.1.call-done
  344.7 1.6 fusion.2
  346.4 0.3 copy.29
  346.6 0.9 reshape.38
  (10 shorter events, 0.2 us)
Async XLA Ops:
  7.2 89.1 %reduce-scatter.3.cloned.1.call-start = ((), (), s32[]{:S(2)}) async-start(), calls=%async_computation.2 | async-start | bytes 3932160 | tf_op jit(solution)/shard_map/reduce_scatter | solution.py:146
  25.1 136.4 %all-gather.2.cloned.1.call-start = ((), (), s32[]{:S(2)}) async-start(), calls=%async_computation.4 | async-start | bytes 3932160 | tf_op jit(solution)/shard_map/all_gather | solution.py:147
  96.3 193.1 %all-reduce.5.cloned.1.call-start = ((), (), s32[]{:S(2)}) async-start(), calls=%async_computation.3 | async-start | bytes 393216 | tf_op jit(solution)/shard_map/psum | solution.py:151
  99.3 245.5 %reduce-scatter.5.cloned.1.call-start = ((), (), s32[]{:S(2)}) async-start(), calls=%async_computation.5 | async-start | bytes 3538944 | tf_op jit(solution)/shard_map/reduce_scatter | solution.py:158
  183.4 159.5 %copy-start = (f32[4,192,256]{2,1,0:T(8,128)S(1)}, f32[4,192,256]{2,1,0:T(8,128)}, u32[]{:S(2)}) copy-start(f32[4,192,256]{2,1,0:T(8,128)} %reduce-scatter.3.cloned.1.call-done) | copy-start | bytes 2359300
Sparse Core Ops, SparseCore 0:
  25.2 71.0 reduce-scatter.2
  97.9 63.5 all-gather.1
  167.5 121.8 all-reduce.4
  292.7 47.3 reduce-scatter.4

commit v2 on v1

--- a/solution.py
+++ b/solution.py
@@ -27,6 +27,7 @@
 
 def sketch_kernel(coords, live, base, tiles_hbm, out, tiles, signs, sems):
     tb = tiles.shape[1]
+    half = tb // 2
     copies = load_tiles(tiles_hbm, tiles, sems)
     for copy in copies:
         copy.start()
@@ -50,9 +51,11 @@
         def step(s, carry):
             i = coords[s, 0]
             j = coords[s, 1]
-            out[i] += lax.dot_general(
+            t = lax.dot_general(
                 signs[j], tiles[s], (((1,), (1,)), ((), ())), preferred_element_type=jnp.float32
             )
+            out[2 * i] += t[:, :half]
+            out[2 * i + 1] += t[:, half:]
             return carry
 
         lax.fori_loop(c * per, jnp.minimum((c + 1) * per, live[0]), step, 0)
@@ -69,7 +72,7 @@
     sketch_copy.wait()
 
     def split(i, carry):
-        x = sketch[i]
+        x = jnp.concatenate([sketch[2 * i], sketch[2 * i + 1]], axis=1)
         for p in range(3):
             y = x.astype(jnp.bfloat16)
             parts[i, p * K : (p + 1) * K, :] = y
@@ -93,6 +96,7 @@
         lax.fori_loop(c * per, jnp.minimum((c + 1) * per, live[0]), step, 0)
 
 
+MESH = pl.DeviceIdType.MESH
 SMEM = pl.BlockSpec(memory_space=pltpu.SMEM)
 VMEM = pl.BlockSpec(memory_space=pltpu.VMEM)
 ANY = pl.BlockSpec(memory_space=pl.ANY)
@@ -102,7 +106,7 @@
     slots, tb, _ = tile_values.shape
     return pl.pallas_call(
         sketch_kernel,
-        out_shape=jax.ShapeDtypeStruct((RT, K, tb), jnp.float32),
+        out_shape=jax.ShapeDtypeStruct((2 * RT, K, tb // 2), jnp.float32),
         in_specs=[SMEM, SMEM, SMEM, ANY],
         out_specs=VMEM,
         scratch_shapes=[
@@ -126,7 +130,7 @@
         out_specs=VMEM,
         scratch_shapes=[
             pltpu.VMEM((slots, tb, tb), jnp.bfloat16),
-            pltpu.VMEM((RT, K, tb), jnp.float32),
+            pltpu.VMEM((2 * RT, K, tb // 2), jnp.float32),
             pltpu.VMEM((RT, 3 * K, tb), jnp.bfloat16),
             pltpu.SemaphoreType.DMA((CHUNKS,)),
             pltpu.SemaphoreType.DMA,
@@ -138,24 +142,302 @@
     )(tile_coords, live_counts, tile_values, sketch_t)
 
 
+def partner_of(index, bit):
+    step = 1 << bit
+    return index + step * (1 - 2 * ((index // step) % 2))
+
+
+def greet(n_col, bits):
+    barrier = pltpu.get_barrier_semaphore()
+    col = lax.axis_index("col")
+    row = lax.axis_index("row")
+    expected = bits
+    for bit in range(bits):
+        pl.semaphore_signal(barrier, inc=1, device_id={"row": partner_of(row, bit)}, device_id_type=MESH)
+    if n_col:
+
+        @pl.when(col > 0)
+        def _():
+            pl.semaphore_signal(barrier, inc=1, device_id={"col": col - 1}, device_id_type=MESH)
+
+        @pl.when(col < n_col - 1)
+        def _():
+            pl.semaphore_signal(barrier, inc=1, device_id={"col": col + 1}, device_id_type=MESH)
+
+        expected = bits + jnp.where(col > 0, 1, 0) + jnp.where(col < n_col - 1, 1, 0)
+    pl.semaphore_wait(barrier, expected)
+
+
+def line_kernel(
+    n_col, bits, part, out, gram, inbox, grams, gram_in, s_red, r_red, s_cast, r_cast, s_gram, r_gram
+):
+    col = lax.axis_index("col")
+    row = lax.axis_index("row")
+    count = part.shape[0] // 2
+    lag = n_col
+    greet(n_col, bits)
+    first = (col == 0, col == n_col - 1)
+    ends = (first[0], first[1])
+    starts = (first[1], first[0])
+    towards = (col - 1, col + 1)
+    away = (col + 1, col - 1)
+
+    def reduce_copy(flow, q, src):
+        return pltpu.make_async_remote_copy(
+            src_ref=src.at[flow * count + q],
+            dst_ref=inbox.at[flow * count + q],
+            send_sem=s_red.at[flow, q],
+            recv_sem=r_red.at[flow, q],
+            device_id={"col": towards[flow]},
+            device_id_type=MESH,
+        )
+
+    def cast_copy(flow, q):
+        return pltpu.make_async_remote_copy(
+            src_ref=out.at[flow * count + q],
+            dst_ref=out.at[flow * count + q],
+            send_sem=s_cast.at[flow, q],
+            recv_sem=r_cast.at[flow, q],
+            device_id={"col": away[flow]},
+            device_id_type=MESH,
+        )
+
+    grams[0] = jnp.zeros_like(grams[0])
+
+    def step(q, carry):
+        @pl.when(q < count)
+        def _():
+            for flow in range(2):
+                b = flow * count + q
+
+                @pl.when(starts[flow])
+                def _():
+                    reduce_copy(flow, q, part).start()
+
+                @pl.when(jnp.logical_not(starts[flow]))
+                def _():
+                    reduce_copy(flow, q, part).wait_recv()
+
+                    @pl.when(ends[flow])
+                    def _():
+                        out[b] = part[b] + inbox[b]
+                        cast_copy(flow, q).start()
+
+                    @pl.when(jnp.logical_not(ends[flow]))
+                    def _():
+                        inbox[b] = part[b] + inbox[b]
+                        reduce_copy(flow, q, inbox).start()
+
+        @pl.when(q >= lag)
+        def _():
+            p = q - lag
+            for flow in range(2):
+
+                @pl.when(jnp.logical_not(ends[flow]))
+                def _():
+                    cast_copy(flow, p).wait_recv()
+
+                    @pl.when(jnp.logical_not(starts[flow]))
+                    def _():
+                        cast_copy(flow, p).start()
+
+            for flow in range(2):
+                x = out[flow * count + p]
+                grams[0] += lax.dot_general(
+                    x, x, (((1,), (1,)), ((), ())), precision=HIGHEST, preferred_element_type=jnp.float32
+                )
+
+        return carry
+
+    lax.fori_loop(0, count + lag, step, 0)
+    for bit in range(bits):
+        copy = pltpu.make_async_remote_copy(
+            src_ref=grams.at[bit],
+            dst_ref=gram_in.at[bit],
+            send_sem=s_gram.at[bit],
+            recv_sem=r_gram.at[bit],
+            device_id={"row": partner_of(row, bit)},
+            device_id_type=MESH,
+        )
+        copy.start()
+        copy.wait()
+        grams[bit + 1] = grams[bit] + gram_in[bit]
+    gram[...] = grams[bits]
+
+    def drain(q, carry):
+        for flow in range(2):
+
+            @pl.when(jnp.logical_not(ends[flow]))
+            def _():
+                reduce_copy(flow, q, part).wait_send()
+
+            @pl.when(jnp.logical_not(starts[flow]))
+            def _():
+                cast_copy(flow, q).wait_send()
+
+        return carry
+
+    lax.fori_loop(0, count, drain, 0)
+
+
+def line_call(n_col, bits, part):
+    blocks = part.shape[0]
+    dma = pltpu.SemaphoreType.DMA
+    return pl.pallas_call(
+        functools.partial(line_kernel, n_col, bits),
+        out_shape=(
+            jax.ShapeDtypeStruct(part.shape, jnp.float32),
+            jax.ShapeDtypeStruct((K, K), jnp.float32),
+        ),
+        in_specs=[VMEM],
+        out_specs=(VMEM, VMEM),
+        scratch_shapes=[
+            pltpu.VMEM(part.shape, jnp.float32),
+            pltpu.VMEM((bits + 1, K, K), jnp.float32),
+            pltpu.VMEM((bits, K, K), jnp.float32),
+            dma((2, blocks // 2)),
+            dma((2, blocks // 2)),
+            dma((2, blocks // 2)),
+            dma((2, blocks // 2)),
+            dma((bits,)),
+            dma((bits,)),
+        ],
+        compiler_params=pltpu.CompilerParams(
+            collective_id=0, has_side_effects=True, vmem_limit_bytes=32 << 20
+        ),
+    )(part)
+
+
+def halving_kernel(bits, part, out, *scratch):
+    inboxes, s_sem, r_sem = scratch[:bits], scratch[bits], scratch[bits + 1]
+    row = lax.axis_index("row")
+    n_row = 1 << bits
+    per = part.shape[0] // n_row
+    kh = K // 2
+    greet(0, bits)
+    orders = (list(range(bits)), [0] + list(range(bits - 1, 0, -1)))
+
+    def bit_of(index, bit):
+        return (index // (1 << bit)) % 2
+
+    def at(level, stream, mine, e):
+        order = orders[stream]
+        value = bit_of(row, order[level])
+        value = value if mine else 1 - value
+        rest = bits - 1 - level
+        if level:
+            return inboxes[level - 1].at[stream, value * (1 << rest) + e]
+        dest = value * (1 << order[0])
+        for i in range(rest):
+            dest = dest + ((e >> (rest - 1 - i)) & 1) * (1 << order[1 + i])
+        return part.at[pl.ds(dest * per, per), pl.ds(stream * kh, kh)]
+
+    def copy_of(level, stream, e):
+        base = sum(1 << (bits - 1 - l) for l in range(level))
+        return pltpu.make_async_remote_copy(
+            src_ref=at(level, stream, False, e),
+            dst_ref=inboxes[level].at[stream, e],
+            send_sem=s_sem.at[stream, base + e],
+            recv_sem=r_sem.at[stream, base + e],
+            device_id={"row": partner_of(row, orders[stream][level])},
+            device_id_type=MESH,
+        )
+
+    sent = []
+    for level in range(bits):
+        slots = range(1 << (bits - 1 - level))
+        copies = [(e, stream, copy_of(level, stream, e)) for e in slots for stream in range(2)]
+        for _, _, copy in copies:
+            copy.start()
+        for e, stream, copy in copies:
+            copy.wait_recv()
+            total = inboxes[level][stream, e] + at(level, stream, True, e)[...]
+            if level < bits - 1:
+                inboxes[level][stream, e] = total
+            else:
+                out[:, stream * kh : (stream + 1) * kh, :] = total
+        sent += copies
+    for _, _, copy in sent:
+        copy.wait_send()
+
+
+def halving_call(bits, part):
+    blocks, _, lanes = part.shape
+    per = blocks >> bits
+    dma = pltpu.SemaphoreType.DMA
+    return pl.pallas_call(
+        functools.partial(halving_kernel, bits),
+        out_shape=jax.ShapeDtypeStruct((per, K, lanes), jnp.float32),
+        in_specs=[VMEM],
+        out_specs=VMEM,
+        scratch_shapes=[
+            pltpu.VMEM((2, 1 << (bits - 1 - level), per, K // 2, lanes), jnp.float32)
+            for level in range(bits)
+        ]
+        + [dma((2, (1 << bits) - 1)), dma((2, (1 << bits) - 1))],
+        compiler_params=pltpu.CompilerParams(
+            collective_id=1, has_side_effects=True, vmem_limit_bytes=32 << 20
+        ),
+    )(part)
+
+
+def dot_nt(a, b):
+    return lax.dot_general(
+        a, b, (((1,), (1,)), ((), ())), precision=HIGHEST, preferred_element_type=jnp.float32
+    )
+
+
+def invert_block(d):
+    b = d.shape[0]
+    rows = lax.broadcasted_iota(jnp.int32, (b, 1), 0)
+    eye = (rows == lax.broadcasted_iota(jnp.int32, (b, b), 1)).astype(jnp.float32)
+    x = jnp.concatenate([d, eye], axis=1)
+    pivots = jnp.zeros((b, 1), jnp.float32)
+    for k in range(b):
+        row = x[k : k + 1, :]
+        pivot = x[k : k + 1, k : k + 1]
+        pivots = jnp.where(rows == k, pivot, pivots)
+        ratio = jnp.where(rows > k, x[:, k : k + 1] / pivot, 0.0)
+        x = x - ratio * row
+    return x[:, b:] * lax.rsqrt(pivots)
+
+
+def factor_kernel(scale, gram, out):
+    b = K // 3
+    g = gram[...]
+    w = scale * (
+        lax.broadcasted_iota(jnp.int32, (K, K), 0) == lax.broadcasted_iota(jnp.int32, (K, K), 1)
+    ).astype(jnp.float32)
+    for p in range(3):
+        inverse = invert_block(g[:b, :b])
+        top = jnp.dot(inverse, w[:b], precision=HIGHEST, preferred_element_type=jnp.float32)
+        out[p * b : (p + 1) * b, :] = top
+        if p < 2:
+            lower = dot_nt(g[b:, :b], inverse)
+            g = g[b:, b:] - dot_nt(lower, lower)
+            w = w[b:] - jnp.dot(lower, top, precision=HIGHEST, preferred_element_type=jnp.float32)
+
+
 def per_device(tile_values, tile_coords, live_counts):
     tb = tile_values.shape[1]
-    base = (lax.axis_index("col") * (CT * tb)).reshape(1)
-    scale = math.sqrt(RT * tb * lax.axis_size("row"))
+    col = lax.axis_index("col")
+    n_col, n_row = lax.axis_size("col"), lax.axis_size("row")
+    bits = n_row.bit_length() - 1
+    base = (col * (CT * tb)).reshape(1)
+    scale = math.sqrt(RT * tb * n_row)
     part = sketch_call(tile_coords, live_counts, base, tile_values)
-    share = lax.psum_scatter(part, "col", scatter_dimension=0, tiled=True)
-    full = lax.all_gather(share, "col", axis=0, tiled=True)
-    gram = jnp.einsum(
-        "bkn,bln->kl", share, share, precision=HIGHEST, preferred_element_type=jnp.float32
-    )
-    gram = lax.psum(gram, ("row", "col"))
-    factor = jnp.linalg.cholesky(gram)
-    inverse = scale * jax.scipy.linalg.solve_triangular(
-        factor, jnp.eye(K, dtype=jnp.float32), lower=True
-    )
+    full, gram = line_call(n_col, bits, part)
+    inverse = pl.pallas_call(
+        functools.partial(factor_kernel, scale),
+        out_shape=jax.ShapeDtypeStruct((K, K), jnp.float32),
+        in_specs=[VMEM],
+        out_specs=VMEM,
+    )(gram)
+    share_blocks = full.shape[0] // n_col
+    share = lax.dynamic_slice_in_dim(full, col * share_blocks, share_blocks, 0)
     basis = jnp.einsum("bkn,lk->bnl", share, inverse, precision=HIGHEST).reshape(-1, K)
     adjoint = adjoint_call(tile_coords, live_counts, tile_values, full)
-    mine = lax.psum_scatter(adjoint, "row", scatter_dimension=0, tiled=True)
+    mine = halving_call(bits, adjoint)
     projected = jnp.einsum("bkn,lk->bnl", mine, inverse, precision=HIGHEST).reshape(1, -1, K)
     return basis, projected
 

time: 355 us -> 550 us (1.55)
  Pallas kernels: 38.3 us -> 542 us
  waiting for transfers between devices: 239 us -> 0 us
  other arithmetic: 49.7 us -> 0 us
  between operations: 15.9 us -> 1.36 us
    pallas_call x1 -> x4, Pallas kernels: 16.4 us -> 525 us  [the longest x1 461 us: line_call(): pl.pallas_call(functools.partial(line_kernel, n_col, bits), out_shape=(ja...]
    psum x1 -> x0, waiting for transfers between devices: 106 us -> none  [per_device(): gram = lax.psum(gram, ('row', 'col'))]
    reduce_scatter x2 -> x0, waiting for transfers between devices: 71.2 us -> none  [the longest x1 71.2 us: per_device(): share = lax.psum_scatter(part, 'col', scatter_dimension=0, tiled=True)]
    all_gather x1 -> x0, waiting for transfers between devices: 62.1 us -> none  [per_device(): full = lax.all_gather(share, 'col', axis=0, tiled=True)]
    another operation x13 -> x0, other arithmetic: 48.7 us -> none  [the longest x7 28.7 us: per_device(): factor = jnp.linalg.cholesky(gram)]
  transfers between devices with their start and end apart: 4 -> 0, of which waited for: 3 -> 0; matrix products, arithmetic and copies ran while one was open for 16% -> 0% of each run, Pallas kernels for 6% -> 0%
where the time goes in v2:
time: 550 us
  Pallas kernels  542 us (99%)
    pallas_call x1, Pallas kernels, line_call(): pl.pallas_call(functools.partial(line_kernel, n_col, bits), out_shape=(ja...  461 us
    pallas_call x1, Pallas kernels, halving_call(): pl.pallas_call(functools.partial(halving_kernel, bits), out_shape=jax.Sha...  30.8 us
    pallas_call x1, Pallas kernels, per_device(): pl.pallas_call(functools.partial(factor_kernel, scale), out_shape=jax.Sha...  20.8 us
    pallas_call x1, Pallas kernels, adjoint_call(): pl.pallas_call(adjoint_kernel, out_shape=jax.ShapeDtypeStruct((2 * CT, K,...  16.9 us
    pallas_call x1, Pallas kernels, sketch_call(): pl.pallas_call(sketch_kernel, out_shape=jax.ShapeDtypeStruct((2 * RT, K,...  11.7 us

profile of v2, /device:TPU:0, one launch (start us, length us, event | category | flops | bytes accessed | tf_op | source)
XLA Modules:
  0.0 549.7 jit_solution(3619870063726872472)
XLA Ops:
  1.3 0.8 copy.7.coords
  2.1 11.7 %shard_map.50.part = f32[32,192,128]{2,1,0:T(8,128)S(1)} custom-call(s32[96,2]{1,0:T(8,128)S(1)} %copy.7.coords, s32[1]{0:T(128)S(6)} %copy.14.live, s32[1]{0:T(128)} %bitcast.base, bf16[96,256,256]{2,1,0:T(8,128)(2,1)} %tiles_hbm.3), custom_call_target="tpu_custom_call" | custom-call | flops 2415919104 | bytes 12582912 | tf_op jit(solution)/shard_map/pallas_call | solution.py:107
  13.8 461.3 %shard_map.51 = (f32[32,192,128]{2,1,0:T(8,128)S(1)}, f32[192,192]{1,0:T(8,128)S(1)}) custom-call(f32[32,192,128]{2,1,0:T(8,128)S(1)} %shard_map.50.part), custom_call_target="tpu_custom_call" | custom-call | tf_op jit(solution)/shard_map/pallas_call | solution.py:286
  475.1 0.0 copy-start
  475.1 0.7 copy-done
  475.8 0.0 copy-start.1
  475.8 20.8 %shard_map.52 = f32[192,192]{1,0:T(8,128)} custom-call(f32[192,192]{1,0:T(8,128)} %copy-done), custom_call_target="tpu_custom_call" | custom-call | tf_op jit(solution)/shard_map/pallas_call | solution.py:430
  496.6 2.7 convolution_bitcast_fusion
  499.2 0.0 copy-done.1
  499.2 16.9 %shard_map.53.part = f32[32,192,128]{2,1,0:T(8,128)S(1)} custom-call(s32[96,2]{1,0:T(8,128)S(1)} %copy.7.coords, s32[1]{0:T(128)S(6)} %copy.14.live, bf16[96,256,256]{2,1,0:T(8,128)(2,1)} %tiles_hbm.3, f32[32,192,128]{2,1,0:T(8,128)} %copy-done.1), custom_call_target="tpu_custom_call" | custom-call | flops 7247757312 | bytes 12582912 | tf_op jit(solution)/shard_map/pallas_call | solution.py:126
  516.2 0.0 copy-start.3
  516.2 0.0 copy-start.2
  516.2 30.8 %shard_map.54 = f32[4,192,128]{2,1,0:T(8,128)S(1)} custom-call(f32[32,192,128]{2,1,0:T(8,128)S(1)} %shard_map.53.part), custom_call_target="tpu_custom_call" | custom-call | tf_op jit(solution)/shard_map/pallas_call | solution.py:368
  547.1 0.0 copy-done.3
  547.1 0.5 fusion.1
  547.6 0.3 copy.10
  547.9 0.9 reshape.15
  548.8 0.0 copy-done.2
  548.8 1.0 copy.13
Async XLA Ops:
  475.1 0.7 copy-start
  475.8 23.4 %copy-start.1 = (f32[32,192,128]{2,1,0:T(8,128)}, f32[32,192,128]{2,1,0:T(8,128)S(1)}, u32[]{:S(2)}) copy-start(f32[32,192,128]{2,1,0:T(8,128)S(1)} %get-tuple-element.4.sketch_hbm) | copy-start | bytes 9437188
  516.2 30.9 %copy-start.3 = (f32[192,192]{1,0:T(8,128)S(1)}, f32[192,192]{1,0:T(8,128)}, u32[]{:S(2)}) copy-start(f32[192,192]{1,0:T(8,128)} %shard_map.52) | copy-start | bytes 442372
  516.2 32.6 %copy-start.2 = (f32[8,24,8,128]{3,2,1,0:T(8,128)S(1)}, f32[8,24,8,128]{3,2,1,0:T(8,128)}, u32[]{:S(2)}) copy-start(f32[8,24,8,128]{3,2,1,0:T(8,128)} %convolution_bitcast_fusion) | copy-start | bytes 2359300

commit v3 on v2

--- a/solution.py
+++ b/solution.py
@@ -12,6 +12,7 @@
 RT = 16
 CT = 16
 CHUNKS = 12
+LAG = 2
 HIGHEST = lax.Precision.HIGHEST
 
 
@@ -174,7 +175,6 @@
     col = lax.axis_index("col")
     row = lax.axis_index("row")
     count = part.shape[0] // 2
-    lag = n_col
     greet(n_col, bits)
     first = (col == 0, col == n_col - 1)
     ends = (first[0], first[1])
@@ -202,37 +202,43 @@
             device_id_type=MESH,
         )
 
+    for flow in range(2):
+
+        @pl.when(starts[flow])
+        def _():
+            def send(q, carry):
+                reduce_copy(flow, q, part).start()
+                return carry
+
+            lax.fori_loop(0, count, send, 0)
+
     grams[0] = jnp.zeros_like(grams[0])
-
-    def step(q, carry):
-        @pl.when(q < count)
-        def _():
-            for flow in range(2):
-                b = flow * count + q
-
-                @pl.when(starts[flow])
+    hops = (n_col - 1 - col, col)
+
+    def step(t, carry):
+        for flow in range(2):
+            q = t - hops[flow] * LAG
+            b = flow * count + q
+
+            @pl.when((q >= 0) & (q < count) & jnp.logical_not(starts[flow]))
+            def _():
+                reduce_copy(flow, q, part).wait_recv()
+
+                @pl.when(ends[flow])
                 def _():
-                    reduce_copy(flow, q, part).start()
-
-                @pl.when(jnp.logical_not(starts[flow]))
+                    out[b] = part[b] + inbox[b]
+                    cast_copy(flow, q).start()
+
+                @pl.when(jnp.logical_not(ends[flow]))
                 def _():
-                    reduce_copy(flow, q, part).wait_recv()
-
-                    @pl.when(ends[flow])
-                    def _():
-                        out[b] = part[b] + inbox[b]
-                        cast_copy(flow, q).start()
-
-                    @pl.when(jnp.logical_not(ends[flow]))
-                    def _():
-                        inbox[b] = part[b] + inbox[b]
-                        reduce_copy(flow, q, inbox).start()
-
-        @pl.when(q >= lag)
-        def _():
-            p = q - lag
-            for flow in range(2):
-
+                    inbox[b] = part[b] + inbox[b]
+                    reduce_copy(flow, q, inbox).start()
+
+        for flow in range(2):
+            p = t - (2 * (n_col - 1) - hops[flow]) * LAG
+
+            @pl.when((p >= 0) & (p < count))
+            def _():
                 @pl.when(jnp.logical_not(ends[flow]))
                 def _():
                     cast_copy(flow, p).wait_recv()
@@ -241,15 +247,12 @@
                     def _():
                         cast_copy(flow, p).start()
 
-            for flow in range(2):
                 x = out[flow * count + p]
-                grams[0] += lax.dot_general(
-                    x, x, (((1,), (1,)), ((), ())), precision=HIGHEST, preferred_element_type=jnp.float32
-                )
+                grams[0] += dot_nt(x, x)
 
         return carry
 
-    lax.fori_loop(0, count + lag, step, 0)
+    lax.fori_loop(0, count + 2 * (n_col - 1) * LAG, step, 0)
     for bit in range(bits):
         copy = pltpu.make_async_remote_copy(
             src_ref=grams.at[bit],
@@ -308,7 +311,7 @@
     )(part)
 
 
-def halving_kernel(bits, part, out, *scratch):
+def halving_kernel(bits, scale, part, gram, out, inverse, *scratch):
     inboxes, s_sem, r_sem = scratch[:bits], scratch[bits], scratch[bits + 1]
     row = lax.axis_index("row")
     n_row = 1 << bits
@@ -343,12 +346,14 @@
             device_id_type=MESH,
         )
 
+    panels = inverse_panels(scale, gram, inverse)
     sent = []
     for level in range(bits):
         slots = range(1 << (bits - 1 - level))
         copies = [(e, stream, copy_of(level, stream, e)) for e in slots for stream in range(2)]
         for _, _, copy in copies:
             copy.start()
+        next(panels, None)
         for e, stream, copy in copies:
             copy.wait_recv()
             total = inboxes[level][stream, e] + at(level, stream, True, e)[...]
@@ -357,19 +362,24 @@
             else:
                 out[:, stream * kh : (stream + 1) * kh, :] = total
         sent += copies
+    for _ in panels:
+        pass
     for _, _, copy in sent:
         copy.wait_send()
 
 
-def halving_call(bits, part):
+def halving_call(bits, scale, part, gram):
     blocks, _, lanes = part.shape
     per = blocks >> bits
     dma = pltpu.SemaphoreType.DMA
     return pl.pallas_call(
-        functools.partial(halving_kernel, bits),
-        out_shape=jax.ShapeDtypeStruct((per, K, lanes), jnp.float32),
-        in_specs=[VMEM],
-        out_specs=VMEM,
+        functools.partial(halving_kernel, bits, scale),
+        out_shape=(
+            jax.ShapeDtypeStruct((per, K, lanes), jnp.float32),
+            jax.ShapeDtypeStruct((K, K), jnp.float32),
+        ),
+        in_specs=[VMEM, VMEM],
+        out_specs=(VMEM, VMEM),
         scratch_shapes=[
             pltpu.VMEM((2, 1 << (bits - 1 - level), per, K // 2, lanes), jnp.float32)
             for level in range(bits)
@@ -378,7 +388,7 @@
         compiler_params=pltpu.CompilerParams(
             collective_id=1, has_side_effects=True, vmem_limit_bytes=32 << 20
         ),
-    )(part)
+    )(part, gram)
 
 
 def dot_nt(a, b):
@@ -402,7 +412,7 @@
     return x[:, b:] * lax.rsqrt(pivots)
 
 
-def factor_kernel(scale, gram, out):
+def inverse_panels(scale, gram, out):
     b = K // 3
     g = gram[...]
     w = scale * (
@@ -416,6 +426,7 @@
             lower = dot_nt(g[b:, :b], inverse)
             g = g[b:, b:] - dot_nt(lower, lower)
             w = w[b:] - jnp.dot(lower, top, precision=HIGHEST, preferred_element_type=jnp.float32)
+        yield
 
 
 def per_device(tile_values, tile_coords, live_counts):
@@ -427,17 +438,11 @@
     scale = math.sqrt(RT * tb * n_row)
     part = sketch_call(tile_coords, live_counts, base, tile_values)
     full, gram = line_call(n_col, bits, part)
-    inverse = pl.pallas_call(
-        functools.partial(factor_kernel, scale),
-        out_shape=jax.ShapeDtypeStruct((K, K), jnp.float32),
-        in_specs=[VMEM],
-        out_specs=VMEM,
-    )(gram)
     share_blocks = full.shape[0] // n_col
     share = lax.dynamic_slice_in_dim(full, col * share_blocks, share_blocks, 0)
+    adjoint = adjoint_call(tile_coords, live_counts, tile_values, full)
+    mine, inverse = halving_call(bits, scale, adjoint, gram)
     basis = jnp.einsum("bkn,lk->bnl", share, inverse, precision=HIGHEST).reshape(-1, K)
-    adjoint = adjoint_call(tile_coords, live_counts, tile_values, full)
-    mine = halving_call(bits, adjoint)
     projected = jnp.einsum("bkn,lk->bnl", mine, inverse, precision=HIGHEST).reshape(1, -1, K)
     return basis, projected
 

time: 550 us -> 211 us (0.38)
  Pallas kernels: 542 us -> 202 us
    pallas_call x1, Pallas kernels: 461 us -> 122 us  [line_call(): pl.pallas_call(functools.partial(line_kernel, n_col, bits), out_shape=(ja...]
    pallas_call x2 -> x1, Pallas kernels: 51.6 us -> 41.1 us  [halving_call(): pl.pallas_call(functools.partial(halving_kernel, bits, scale), out_shape=...]
    pallas_call x1, Pallas kernels: 16.9 us -> 22.7 us  [adjoint_call(): pl.pallas_call(adjoint_kernel, out_shape=jax.ShapeDtypeStruct((2 * CT, K,...]
where the time goes in v3:
time: 211 us
  Pallas kernels  202 us (96%)
  local copies, waits for them, and re-layouts  4.55 us (2%)
  matrix products  2.5 us (1%)
    pallas_call x1, Pallas kernels, line_call(): pl.pallas_call(functools.partial(line_kernel, n_col, bits), out_shape=(ja...  122 us
    pallas_call x1, Pallas kernels, halving_call(): pl.pallas_call(functools.partial(halving_kernel, bits, scale), out_shape=...  41.1 us
    pallas_call x1, Pallas kernels, adjoint_call(): pl.pallas_call(adjoint_kernel, out_shape=jax.ShapeDtypeStruct((2 * CT, K,...  22.7 us
    pallas_call x1, Pallas kernels, sketch_call(): pl.pallas_call(sketch_kernel, out_shape=jax.ShapeDtypeStruct((2 * RT, K,...  16.9 us

profile of v3, /device:TPU:0, one launch (start us, length us, event | category | flops | bytes accessed | tf_op | source)
XLA Modules:
  0.0 210.7 jit_solution(5355527199725601113)
XLA Ops:
  1.3 0.8 copy.7.coords
  2.1 16.9 %shard_map.50.part = f32[32,192,128]{2,1,0:T(8,128)S(1)} custom-call(s32[96,2]{1,0:T(8,128)S(1)} %copy.7.coords, s32[1]{0:T(128)S(6)} %copy.14.live, s32[1]{0:T(128)} %bitcast.base, bf16[96,256,256]{2,1,0:T(8,128)(2,1)} %tiles_hbm.3), custom_call_target="tpu_custom_call" | custom-call | flops 2415919104 | bytes 12582912 | tf_op jit(solution)/shard_map/pallas_call | solution.py:108
  18.9 121.6 %shard_map.51 = (f32[32,192,128]{2,1,0:T(8,128)S(1)}, f32[192,192]{1,0:T(8,128)S(1)}) custom-call(f32[32,192,128]{2,1,0:T(8,128)S(1)} %shard_map.50.part), custom_call_target="tpu_custom_call" | custom-call | tf_op jit(solution)/shard_map/pallas_call | solution.py:289
  140.6 0.0 copy-start
  140.6 1.6 copy-done
  142.2 22.7 %shard_map.52.part = f32[32,192,128]{2,1,0:T(8,128)S(1)} custom-call(s32[96,2]{1,0:T(8,128)S(1)} %copy.7.coords, s32[1]{0:T(128)S(6)} %copy.14.live, bf16[96,256,256]{2,1,0:T(8,128)(2,1)} %tiles_hbm.3, f32[32,192,128]{2,1,0:T(8,128)} %copy-done), custom_call_target="tpu_custom_call" | custom-call | flops 7247757312 | bytes 12582912 | tf_op jit(solution)/shard_map/pallas_call | solution.py:127
  164.9 41.1 %shard_map.53 = (f32[4,192,128]{2,1,0:T(8,128)S(1)}, f32[192,192]{1,0:T(8,128)S(1)}) custom-call(f32[32,192,128]{2,1,0:T(8,128)S(1)} %shard_map.52.part, f32[192,192]{1,0:T(8,128)S(1)} %get-tuple-element.7.gram), custom_call_target="tpu_custom_call" | custom-call | tf_op jit(solution)/shard_map/pallas_call | solution.py:375
  206.1 2.0 convolution_bitcast_fusion
  208.0 0.5 fusion.1
  208.6 0.3 copy.10
  208.8 0.9 reshape.15
  209.7 1.0 copy.13
Async XLA Ops:
  140.6 1.7 copy-start

commit v4 on v3

--- a/solution.py
+++ b/solution.py
@@ -62,25 +62,15 @@
         lax.fori_loop(c * per, jnp.minimum((c + 1) * per, live[0]), step, 0)
 
 
-def adjoint_kernel(coords, live, tiles_hbm, sketch_hbm, out, tiles, sketch, parts, sems, sketch_sem):
+def adjoint_kernel(coords, live, tiles_hbm, parts_hbm, out, tiles, parts, sems, parts_sem):
     half = out.shape[2]
-    sketch_copy = pltpu.make_async_copy(sketch_hbm, sketch, sketch_sem)
-    sketch_copy.start()
+    parts_copy = pltpu.make_async_copy(parts_hbm, parts, parts_sem)
+    parts_copy.start()
     copies = load_tiles(tiles_hbm, tiles, sems)
     for copy in copies:
         copy.start()
     out[...] = jnp.zeros_like(out)
-    sketch_copy.wait()
-
-    def split(i, carry):
-        x = jnp.concatenate([sketch[2 * i], sketch[2 * i + 1]], axis=1)
-        for p in range(3):
-            y = x.astype(jnp.bfloat16)
-            parts[i, p * K : (p + 1) * K, :] = y
-            x = x - y.astype(jnp.float32)
-        return carry
-
-    lax.fori_loop(0, RT, split, 0)
+    parts_copy.wait()
     per = tiles.shape[0] // CHUNKS
     for c, copy in enumerate(copies):
         copy.wait()
@@ -122,7 +112,7 @@
     )(tile_coords, live_counts, base, tile_values)
 
 
-def adjoint_call(tile_coords, live_counts, tile_values, sketch_t):
+def adjoint_call(tile_coords, live_counts, tile_values, parts):
     slots, tb, _ = tile_values.shape
     return pl.pallas_call(
         adjoint_kernel,
@@ -131,8 +121,7 @@
         out_specs=VMEM,
         scratch_shapes=[
             pltpu.VMEM((slots, tb, tb), jnp.bfloat16),
-            pltpu.VMEM((2 * RT, K, tb // 2), jnp.float32),
-            pltpu.VMEM((RT, 3 * K, tb), jnp.bfloat16),
+            pltpu.VMEM(parts.shape, jnp.bfloat16),
             pltpu.SemaphoreType.DMA((CHUNKS,)),
             pltpu.SemaphoreType.DMA,
         ],
@@ -140,7 +129,7 @@
         cost_estimate=pl.CostEstimate(
             flops=6 * slots * tb * tb * K, bytes_accessed=slots * tb * tb * 2, transcendentals=0
         ),
-    )(tile_coords, live_counts, tile_values, sketch_t)
+    )(tile_coords, live_counts, tile_values, parts)
 
 
 def partner_of(index, bit):
@@ -170,7 +159,24 @@
 
 
 def line_kernel(
-    n_col, bits, part, out, gram, inbox, grams, gram_in, s_red, r_red, s_cast, r_cast, s_gram, r_gram
+    n_col,
+    bits,
+    part,
+    out,
+    parts,
+    gram,
+    inbox,
+    products,
+    squares,
+    halves,
+    grams,
+    gram_in,
+    s_red,
+    r_red,
+    s_cast,
+    r_cast,
+    s_gram,
+    r_gram,
 ):
     col = lax.axis_index("col")
     row = lax.axis_index("row")
@@ -212,7 +218,8 @@
 
             lax.fori_loop(0, count, send, 0)
 
-    grams[0] = jnp.zeros_like(grams[0])
+    products[...] = jnp.zeros_like(products)
+    squares[...] = jnp.zeros_like(squares)
     hops = (n_col - 1 - col, col)
 
     def step(t, carry):
@@ -247,25 +254,49 @@
                     def _():
                         cast_copy(flow, p).start()
 
-                x = out[flow * count + p]
-                grams[0] += dot_nt(x, x)
+                @pl.when(p % 2 == 1)
+                def _():
+                    b = flow * count + p
+                    x = jnp.concatenate([out[b - 1], out[b]], axis=1)
+                    high = x.astype(jnp.bfloat16)
+                    x = x - high.astype(jnp.float32)
+                    middle = x.astype(jnp.bfloat16)
+                    low = (x - middle.astype(jnp.float32)).astype(jnp.bfloat16)
+                    terms = jnp.concatenate([high, middle, low], axis=0)
+                    parts[b // 2] = terms
+                    products[...] += narrow_nt(terms, high)
+                    squares[...] += narrow_nt(middle, middle)
 
         return carry
 
     lax.fori_loop(0, count + 2 * (n_col - 1) * LAG, step, 0)
-    for bit in range(bits):
-        copy = pltpu.make_async_remote_copy(
-            src_ref=grams.at[bit],
-            dst_ref=gram_in.at[bit],
-            send_sem=s_gram.at[bit],
-            recv_sem=r_gram.at[bit],
+    cross = products[K : 2 * K] + products[2 * K :]
+    total = products[:K] + squares[...] + cross + cross.T
+    halves[0] = total[: K // 2]
+    halves[1] = total[K // 2 :]
+    core = row % 2
+
+    def gram_copy(step, src, dst, bit):
+        return pltpu.make_async_remote_copy(
+            src_ref=src,
+            dst_ref=dst,
+            send_sem=s_gram.at[step],
+            recv_sem=r_gram.at[step],
             device_id={"row": partner_of(row, bit)},
             device_id_type=MESH,
         )
+
+    for bit in range(bits):
+        src = grams.at[bit - 1] if bit else halves.at[1 - core]
+        copy = gram_copy(bit, src, gram_in.at[bit], bit)
         copy.start()
         copy.wait()
-        grams[bit + 1] = grams[bit] + gram_in[bit]
-    gram[...] = grams[bits]
+        grams[bit] = (grams[bit - 1] if bit else halves[core]) + gram_in[bit]
+    copy = gram_copy(bits, grams.at[bits - 1], gram_in.at[bits], 0)
+    copy.start()
+    copy.wait()
+    gram[pl.ds(pl.multiple_of(core * (K // 2), 8), K // 2), :] = grams[bits - 1]
+    gram[pl.ds(pl.multiple_of((1 - core) * (K // 2), 8), K // 2), :] = gram_in[bits]
 
     def drain(q, carry):
         for flow in range(2):
@@ -290,20 +321,24 @@
         functools.partial(line_kernel, n_col, bits),
         out_shape=(
             jax.ShapeDtypeStruct(part.shape, jnp.float32),
+            jax.ShapeDtypeStruct((RT, 3 * K, 2 * part.shape[2]), jnp.bfloat16),
             jax.ShapeDtypeStruct((K, K), jnp.float32),
         ),
         in_specs=[VMEM],
-        out_specs=(VMEM, VMEM),
+        out_specs=(VMEM, VMEM, VMEM),
         scratch_shapes=[
             pltpu.VMEM(part.shape, jnp.float32),
-            pltpu.VMEM((bits + 1, K, K), jnp.float32),
-            pltpu.VMEM((bits, K, K), jnp.float32),
+            pltpu.VMEM((3 * K, K), jnp.float32),
+            pltpu.VMEM((K, K), jnp.float32),
+            pltpu.VMEM((2, K // 2, K), jnp.float32),
+            pltpu.VMEM((bits, K // 2, K), jnp.float32),
+            pltpu.VMEM((bits + 1, K // 2, K), jnp.float32),
             dma((2, blocks // 2)),
             dma((2, blocks // 2)),
             dma((2, blocks // 2)),
             dma((2, blocks // 2)),
-            dma((bits,)),
-            dma((bits,)),
+            dma((bits + 1,)),
+            dma((bits + 1,)),
         ],
         compiler_params=pltpu.CompilerParams(
             collective_id=0, has_side_effects=True, vmem_limit_bytes=32 << 20
@@ -391,6 +426,10 @@
     )(part, gram)
 
 
+def narrow_nt(a, b):
+    return lax.dot_general(a, b, (((1,), (1,)), ((), ())), preferred_element_type=jnp.float32)
+
+
 def dot_nt(a, b):
     return lax.dot_general(
         a, b, (((1,), (1,)), ((), ())), precision=HIGHEST, preferred_element_type=jnp.float32
@@ -402,14 +441,18 @@
     rows = lax.broadcasted_iota(jnp.int32, (b, 1), 0)
     eye = (rows == lax.broadcasted_iota(jnp.int32, (b, b), 1)).astype(jnp.float32)
     x = jnp.concatenate([d, eye], axis=1)
-    pivots = jnp.zeros((b, 1), jnp.float32)
-    for k in range(b):
-        row = x[k : k + 1, :]
-        pivot = x[k : k + 1, k : k + 1]
-        pivots = jnp.where(rows == k, pivot, pivots)
-        ratio = jnp.where(rows > k, x[:, k : k + 1] / pivot, 0.0)
-        x = x - ratio * row
-    return x[:, b:] * lax.rsqrt(pivots)
+    pivots = jnp.ones_like(x)
+    for start in range(0, b, 4):
+        columns = [jnp.broadcast_to(x[:, k : k + 1], x.shape) for k in range(start, start + 4)]
+        for i in range(4):
+            k = start + i
+            pivot = columns[i][k : k + 1, :]
+            pivots = jnp.where(rows == k, pivot, pivots)
+            ratio = jnp.where(rows > k, columns[i] * (1.0 / pivot), 0.0)
+            for j in range(i + 1, 4):
+                columns[j] = columns[j] - ratio * columns[j][k : k + 1, :]
+            x = x - ratio * x[k : k + 1, :]
+    return x[:, b:] * lax.rsqrt(pivots)[:, b:]
 
 
 def inverse_panels(scale, gram, out):
@@ -437,10 +480,10 @@
     base = (col * (CT * tb)).reshape(1)
     scale = math.sqrt(RT * tb * n_row)
     part = sketch_call(tile_coords, live_counts, base, tile_values)
-    full, gram = line_call(n_col, bits, part)
+    full, parts, gram = line_call(n_col, bits, part)
     share_blocks = full.shape[0] // n_col
     share = lax.dynamic_slice_in_dim(full, col * share_blocks, share_blocks, 0)
-    adjoint = adjoint_call(tile_coords, live_counts, tile_values, full)
+    adjoint = adjoint_call(tile_coords, live_counts, tile_values, parts)
     mine, inverse = halving_call(bits, scale, adjoint, gram)
     basis = jnp.einsum("bkn,lk->bnl", share, inverse, precision=HIGHEST).reshape(-1, K)
     projected = jnp.einsum("bkn,lk->bnl", mine, inverse, precision=HIGHEST).reshape(1, -1, K)

time: 211 us -> 200 us (0.948)
  Pallas kernels: 202 us -> 194 us
    pallas_call x1, Pallas kernels: 22.7 us -> 14.7 us  [adjoint_call(): pl.pallas_call(adjoint_kernel, out_shape=jax.ShapeDtypeStruct((2 * CT, K,...]
    pallas_call x1, Pallas kernels: 16.9 us -> 10 us  [sketch_call(): pl.pallas_call(sketch_kernel, out_shape=jax.ShapeDtypeStruct((2 * RT, K,...]
    pallas_call x1, Pallas kernels: 122 us -> 125 us  [line_call(): pl.pallas_call(functools.partial(line_kernel, n_col, bits), out_shape=(ja...]
    pallas_call x1, Pallas kernels: 41.1 us -> 43.7 us  [halving_call(): pl.pallas_call(functools.partial(halving_kernel, bits, scale), out_shape=...]
where the time goes in v4:
time: 200 us; the launch traced here: 201 us
  Pallas kernels  194 us (97%)
  local copies, waits for them, and re-layouts  5.02 us (3%)
    pallas_call x1, Pallas kernels, line_call(): pl.pallas_call(functools.partial(line_kernel, n_col, bits), out_shape=(ja...  125 us
    pallas_call x1, Pallas kernels, halving_call(): pl.pallas_call(functools.partial(halving_kernel, bits, scale), out_shape=...  43.7 us
    pallas_call x1, Pallas kernels, adjoint_call(): pl.pallas_call(adjoint_kernel, out_shape=jax.ShapeDtypeStruct((2 * CT, K,...  14.7 us
    pallas_call x1, Pallas kernels, sketch_call(): pl.pallas_call(sketch_kernel, out_shape=jax.ShapeDtypeStruct((2 * RT, K,...  10 us

profile of v4, /device:TPU:0, one launch (start us, length us, event | category | flops | bytes accessed | tf_op | source)
XLA Modules:
  0.0 201.4 jit_solution(2970853207434962132)
XLA Ops:
  1.3 0.8 copy.7.coords
  2.1 10.0 %shard_map.50.part = f32[32,192,128]{2,1,0:T(8,128)S(1)} custom-call(s32[96,2]{1,0:T(8,128)S(1)} %copy.7.coords, s32[1]{0:T(128)S(6)} %copy.14.live, s32[1]{0:T(128)} %bitcast.base, bf16[96,256,256]{2,1,0:T(8,128)(2,1)} %tiles_hbm.3), custom_call_target="tpu_custom_call" | custom-call | flops 2415919104 | bytes 12582912 | tf_op jit(solution)/shard_map/pallas_call | solution.py:98
  12.1 125.3 %shard_map.51 = (f32[32,192,128]{2,1,0:T(8,128)S(1)}, bf16[16,576,256]{2,1,0:T(8,128)(2,1)S(1)}, f32[192,192]{1,0:T(8,128)S(1)}) custom-call(f32[32,192,128]{2,1,0:T(8,128)S(1)} %shard_map.50.part), custom_call_target="tpu_custom_call" | custom-call | tf_op jit(solution)/shard_map/pallas_call | solution.py:320
  137.4 0.0 copy-start
  137.4 2.1 %copy-done = bf16[16,576,256]{2,1,0:T(8,128)(2,1)} copy-done((bf16[16,576,256]{2,1,0:T(8,128)(2,1)}, bf16[16,576,256]{2,1,0:T(8,128)(2,1)S(1)}, u32[]{:S(2)}) %copy-start) | copy-done | bytes 4718616
  139.5 14.7 %shard_map.52.part = f32[32,192,128]{2,1,0:T(8,128)S(1)} custom-call(s32[96,2]{1,0:T(8,128)S(1)} %copy.7.coords, s32[1]{0:T(128)S(6)} %copy.14.live, bf16[96,256,256]{2,1,0:T(8,128)(2,1)} %tiles_hbm.3, bf16[16,576,256]{2,1,0:T(8,128)(2,1)} %copy-done), custom_call_target="tpu_custom_call" | custom-call | flops 7247757312 | bytes 12582912 | tf_op jit(solution)/shard_map/pallas_call | solution.py:117
  154.2 43.7 %shard_map.53 = (f32[4,192,128]{2,1,0:T(8,128)S(1)}, f32[192,192]{1,0:T(8,128)S(1)}) custom-call(f32[32,192,128]{2,1,0:T(8,128)S(1)} %shard_map.52.part, f32[192,192]{1,0:T(8,128)S(1)} %get-tuple-element.9.gram), custom_call_target="tpu_custom_call" | custom-call | tf_op jit(solution)/shard_map/pallas_call | solution.py:410
  197.9 0.9 convolution_bitcast_fusion
  198.8 0.5 fusion.1
  199.3 0.3 copy.10
  199.6 0.9 reshape.15
  200.5 1.0 copy.13
Async XLA Ops:
  137.4 2.1 %copy-start = (bf16[16,576,256]{2,1,0:T(8,128)(2,1)}, bf16[16,576,256]{2,1,0:T(8,128)(2,1)S(1)}, u32[]{:S(2)}) copy-start(bf16[16,576,256]{2,1,0:T(8,128)(2,1)S(1)} %get-tuple-element.8.parts_hbm) | copy-start | bytes 14155780

commit v5 on v4

--- a/solution.py
+++ b/solution.py
@@ -12,7 +12,7 @@
 RT = 16
 CT = 16
 CHUNKS = 12
-LAG = 2
+LAG = 3
 HIGHEST = lax.Precision.HIGHEST
 
 
@@ -49,17 +49,23 @@
     for c, copy in enumerate(copies):
         copy.wait()
 
-        def step(s, carry):
-            i = coords[s, 0]
-            j = coords[s, 1]
-            t = lax.dot_general(
-                signs[j], tiles[s], (((1,), (1,)), ((), ())), preferred_element_type=jnp.float32
-            )
-            out[2 * i] += t[:, :half]
-            out[2 * i + 1] += t[:, half:]
+        def step(group, carry):
+            terms = []
+            for s in range(4):
+                s = group * 4 + s
+                t = lax.dot_general(
+                    signs[coords[s, 1]],
+                    tiles[s],
+                    (((1,), (1,)), ((), ())),
+                    preferred_element_type=jnp.float32,
+                )
+                terms.append((coords[s, 0], jnp.where(s < live[0], t, 0.0)))
+            for i, t in terms:
+                out[2 * i] += t[:, :half]
+                out[2 * i + 1] += t[:, half:]
             return carry
 
-        lax.fori_loop(c * per, jnp.minimum((c + 1) * per, live[0]), step, 0)
+        lax.fori_loop(c * per // 4, jnp.minimum((c + 1) * per, live[0] + 3) // 4, step, 0)
 
 
 def adjoint_kernel(coords, live, tiles_hbm, parts_hbm, out, tiles, parts, sems, parts_sem):
@@ -75,16 +81,19 @@
     for c, copy in enumerate(copies):
         copy.wait()
 
-        def step(s, carry):
-            i = coords[s, 0]
-            j = coords[s, 1]
-            t = jnp.dot(parts[i], tiles[s], preferred_element_type=jnp.float32)
-            t = t[:K] + t[K : 2 * K] + t[2 * K :]
-            out[2 * j] += t[:, :half]
-            out[2 * j + 1] += t[:, half:]
+        def step(group, carry):
+            terms = []
+            for s in range(4):
+                s = group * 4 + s
+                t = jnp.dot(parts[coords[s, 0]], tiles[s], preferred_element_type=jnp.float32)
+                t = t[:K] + t[K : 2 * K] + t[2 * K :]
+                terms.append((coords[s, 1], jnp.where(s < live[0], t, 0.0)))
+            for j, t in terms:
+                out[2 * j] += t[:, :half]
+                out[2 * j + 1] += t[:, half:]
             return carry
 
-        lax.fori_loop(c * per, jnp.minimum((c + 1) * per, live[0]), step, 0)
+        lax.fori_loop(c * per // 4, jnp.minimum((c + 1) * per, live[0] + 3) // 4, step, 0)
 
 
 MESH = pl.DeviceIdType.MESH
@@ -162,9 +171,10 @@
     n_col,
     bits,
     part,
-    out,
+    share,
     parts,
     gram,
+    out,
     inbox,
     products,
     squares,
@@ -254,16 +264,18 @@
                     def _():
                         cast_copy(flow, p).start()
 
-                @pl.when(p % 2 == 1)
+                @pl.when(p % 4 == 3)
                 def _():
                     b = flow * count + p
-                    x = jnp.concatenate([out[b - 1], out[b]], axis=1)
+                    left = jnp.concatenate([out[b - 3], out[b - 2]], axis=0)
+                    right = jnp.concatenate([out[b - 1], out[b]], axis=0)
+                    x = jnp.concatenate([left, right], axis=1)
                     high = x.astype(jnp.bfloat16)
                     x = x - high.astype(jnp.float32)
                     middle = x.astype(jnp.bfloat16)
                     low = (x - middle.astype(jnp.float32)).astype(jnp.bfloat16)
                     terms = jnp.concatenate([high, middle, low], axis=0)
-                    parts[b // 2] = terms
+                    parts[b // 4] = terms
                     products[...] += narrow_nt(terms, high)
                     squares[...] += narrow_nt(middle, middle)
 
@@ -298,6 +310,9 @@
     gram[pl.ds(pl.multiple_of(core * (K // 2), 8), K // 2), :] = grams[bits - 1]
     gram[pl.ds(pl.multiple_of((1 - core) * (K // 2), 8), K // 2), :] = gram_in[bits]
 
+    own = share.shape[0]
+    share[...] = out[pl.ds(col * own, own)]
+
     def drain(q, carry):
         for flow in range(2):
 
@@ -320,13 +335,14 @@
     return pl.pallas_call(
         functools.partial(line_kernel, n_col, bits),
         out_shape=(
-            jax.ShapeDtypeStruct(part.shape, jnp.float32),
+            jax.ShapeDtypeStruct((blocks // n_col,) + part.shape[1:], jnp.float32),
             jax.ShapeDtypeStruct((RT, 3 * K, 2 * part.shape[2]), jnp.bfloat16),
             jax.ShapeDtypeStruct((K, K), jnp.float32),
         ),
         in_specs=[VMEM],
         out_specs=(VMEM, VMEM, VMEM),
         scratch_shapes=[
+            pltpu.VMEM(part.shape, jnp.float32),
             pltpu.VMEM(part.shape, jnp.float32),
             pltpu.VMEM((3 * K, K), jnp.float32),
             pltpu.VMEM((K, K), jnp.float32),
@@ -480,9 +496,9 @@
     base = (col * (CT * tb)).reshape(1)
     scale = math.sqrt(RT * tb * n_row)
     part = sketch_call(tile_coords, live_counts, base, tile_values)
-    full, parts, gram = line_call(n_col, bits, part)
-    share_blocks = full.shape[0] // n_col
-    share = lax.dynamic_slice_in_dim(full, col * share_blocks, share_blocks, 0)
+    lanes = part.shape[2]
+    share, parts, gram = line_call(n_col, bits, part.reshape(-1, K // 2, lanes))
+    share = share.reshape(-1, K, lanes)
     adjoint = adjoint_call(tile_coords, live_counts, tile_values, parts)
     mine, inverse = halving_call(bits, scale, adjoint, gram)
     basis = jnp.einsum("bkn,lk->bnl", share, inverse, precision=HIGHEST).reshape(-1, K)

time: 200 us -> 181 us (0.905)
  Pallas kernels: 194 us -> 173 us
    pallas_call x1, Pallas kernels: 43.7 us -> 28.7 us  [halving_call(): pl.pallas_call(functools.partial(halving_kernel, bits, scale), out_shape=...]
    pallas_call x1, Pallas kernels: 125 us -> 117 us  [line_call(): pl.pallas_call(functools.partial(line_kernel, n_col, bits), out_shape=(ja...]
    pallas_call x1, Pallas kernels: 14.7 us -> 17.3 us  [adjoint_call(): pl.pallas_call(adjoint_kernel, out_shape=jax.ShapeDtypeStruct((2 * CT, K,...]
where the time goes in v5:
time: 181 us
  Pallas kernels  173 us (96%)
  local copies, waits for them, and re-layouts  4.5 us (2%)
  matrix products  2.34 us (1%)
    pallas_call x1, Pallas kernels, line_call(): pl.pallas_call(functools.partial(line_kernel, n_col, bits), out_shape=(ja...  117 us
    pallas_call x1, Pallas kernels, halving_call(): pl.pallas_call(functools.partial(halving_kernel, bits, scale), out_shape=...  28.7 us
    pallas_call x1, Pallas kernels, adjoint_call(): pl.pallas_call(adjoint_kernel, out_shape=jax.ShapeDtypeStruct((2 * CT, K,...  17.3 us
    pallas_call x1, Pallas kernels, sketch_call(): pl.pallas_call(sketch_kernel, out_shape=jax.ShapeDtypeStruct((2 * RT, K,...  10.3 us

profile of v5, /device:TPU:0, one launch (start us, length us, event | category | flops | bytes accessed | tf_op | source)
XLA Modules:
  0.0 181.1 jit_solution(12617350187303190105)
XLA Ops:
  1.3 0.8 copy.7.coords
  2.1 10.3 %shard_map.50 = f32[32,192,128]{2,1,0:T(8,128)S(1)} custom-call(s32[96,2]{1,0:T(8,128)S(1)} %copy.7.coords, s32[1]{0:T(128)S(6)} %copy.16.live, s32[1]{0:T(128)} %bitcast.base, bf16[96,256,256]{2,1,0:T(8,128)(2,1)} %tiles_hbm.3), custom_call_target="tpu_custom_call" | custom-call | flops 2415919104 | bytes 12582912 | tf_op jit(solution)/shard_map/pallas_call | solution.py:107
  12.4 116.6 %shard_map.51 = (f32[16,96,128]{2,1,0:T(8,128)S(1)}, bf16[16,576,256]{2,1,0:T(8,128)(2,1)S(1)}, f32[192,192]{1,0:T(8,128)S(1)}) custom-call(f32[64,96,128]{2,1,0:T(8,128)S(1)} %bitcast.17), custom_call_target="tpu_custom_call" | custom-call | tf_op jit(solution)/shard_map/pallas_call | solution.py:335
  129.0 0.0 copy-start
  129.0 2.1 %copy-done = bf16[16,576,256]{2,1,0:T(8,128)(2,1)} copy-done((bf16[16,576,256]{2,1,0:T(8,128)(2,1)}, bf16[16,576,256]{2,1,0:T(8,128)(2,1)S(1)}, u32[]{:S(2)}) %copy-start) | copy-done | bytes 4718616
  131.1 0.5 copy.8
  131.6 17.3 %shard_map.52.part = f32[32,192,128]{2,1,0:T(8,128)S(1)} custom-call(s32[96,2]{1,0:T(8,128)S(1)} %copy.7.coords, s32[1]{0:T(128)S(6)} %copy.16.live, bf16[96,256,256]{2,1,0:T(8,128)(2,1)} %tiles_hbm.3, bf16[16,576,256]{2,1,0:T(8,128)(2,1)} %copy-done), custom_call_target="tpu_custom_call" | custom-call | flops 7247757312 | bytes 12582912 | tf_op jit(solution)/shard_map/pallas_call | solution.py:126
  148.9 28.7 %shard_map.53 = (f32[4,192,128]{2,1,0:T(8,128)S(1)}, f32[192,192]{1,0:T(8,128)S(1)}) custom-call(f32[32,192,128]{2,1,0:T(8,128)S(1)} %shard_map.52.part, f32[192,192]{1,0:T(8,128)S(1)} %get-tuple-element.9.gram), custom_call_target="tpu_custom_call" | custom-call | tf_op jit(solution)/shard_map/pallas_call | solution.py:426
  177.6 0.5 fusion.3
  178.1 1.8 %fusion = f32[1024,192]{0,1:T(8,128)} fusion(f32[192,192]{1,0:T(8,128)S(1)} %get-tuple-element.10, f32[24,8,8,128]{3,2,1,0:T(8,128)S(1)} %bitcast.19), kind=kOutput, calls=%fused_computation | convolution fusion | flops 452984832 | bytes 1720320 | tf_op jit(solution)/shard_map/bkn,lk->bnl/dot_general | solution.py:504
  179.9 0.3 copy.10
  180.2 0.9 reshape.21
Async XLA Ops:
  129.0 2.1 %copy-start = (bf16[16,576,256]{2,1,0:T(8,128)(2,1)}, bf16[16,576,256]{2,1,0:T(8,128)(2,1)S(1)}, u32[]{:S(2)}) copy-start(bf16[16,576,256]{2,1,0:T(8,128)(2,1)S(1)} %get-tuple-element.8.parts_hbm) | copy-start | bytes 14155780
